TPU v7x, 32 devices: a whole 2x2x4 slice. The times are simulated.
32 devices in a mesh: trial: 4 (over y, x), dp: 8 (over z, core).
Axes of the slice: x: 2, y: 2, z: 4, core: 2. Of those that a mesh axis runs over, the one named last changes fastest.
Arguments:
- grads: bfloat16 [32, 4, 512, 512], P(('trial', 'dp')), may hold values from -75 to 75
- exponents: int32 [8], replicated, may hold values from 2 to 4
- dampings: float32 [8], replicated, may hold values from 0.05 to 0.5
Outputs:
- updates: bfloat16 [8, 4, 512, 512], P(None, None, 'dp', 'trial')
All inputs are finite; a program needn't handle non-finite values.
Results may differ from a plain program's by a relative error of at most 0.0004.
Values may be sent and summed in bfloat16 or wider, within the bound.
A program may use at most 128 MiB of HBM per device.

v0:
```python
from functools import partial

import jax
import jax.numpy as jnp
from jax import lax
from jax.sharding import PartitionSpec as P

ITERS = 2


def from_behind(block, axis, distance):
    devices = range(lax.axis_size(axis))
    route = [(i - distance, i) for i in devices if i - distance in devices]
    return lax.ppermute(block, axis, route)


def matmul_full(first_mat, second_mat):
    return jnp.matmul(first_mat, second_mat, precision=lax.Precision.HIGHEST)


def inverse_root(statistic, exponent, damping):
    identity = jnp.eye(statistic.shape[-1], dtype=jnp.float32)
    shifted = statistic + damping * identity
    order_f = exponent.astype(jnp.float32)
    scaling = (1.0 + order_f) / (2.0 * jnp.sqrt(jnp.sum(shifted * shifted) + 1e-06))
    moment = scaling * shifted
    root_now = jnp.exp(jnp.log(scaling) / order_f) * identity
    for iteration in range(ITERS):
        factor = ((order_f + 1.0) * identity - moment) / order_f
        root_now = matmul_full(root_now, factor)
        if iteration + 1 < ITERS:
            raised = lax.fori_loop(
                1, exponent, lambda turn, product: matmul_full(product, factor), factor
            )
            moment = matmul_full(raised, moment)
    return root_now


def graft(raw_update, average):
    target = jnp.sqrt(jnp.mean(average * average, axis=(-2, -1), keepdims=True))
    spread = jnp.sqrt(jnp.mean(raw_update * raw_update, axis=(-2, -1), keepdims=True) + 1e-06)
    return raw_update * target / spread


def row_term(grad_tiles, kind_index, stat_weight, mean_weight, row_start, row_count):
    if kind_index == 0:
        band = grad_tiles
        return (
            jnp.einsum("nrk,nck->rnc", band, grad_tiles, preferred_element_type=jnp.float32)
            * stat_weight
        )
    if kind_index == 1:
        band = grad_tiles
        return (
            jnp.einsum("nkr,nkc->rnc", band, grad_tiles, preferred_element_type=jnp.float32)
            * stat_weight
        )
    band = grad_tiles
    return band.transpose(1, 0, 2).astype(jnp.float32) * mean_weight


def per_device(grads, exponents, dampings):
    grad_tiles = grads[0]
    tile_count = grad_tiles.shape[0]
    block_order = grad_tiles.shape[1]
    trials_n = lax.axis_size("trial")
    data_n = lax.axis_size("dp")
    devices = trials_n * data_n
    row_share = block_order // data_n
    col_share = block_order // trials_n
    here_trial = lax.axis_index("trial")
    here_data = lax.axis_index("dp")
    worker = here_trial * data_n + here_data
    task_count = exponents.shape[0] * tile_count
    stat_weight = 1.0 / (devices * block_order)
    mean_weight = 1.0 / devices
    unit_count = 2 * task_count
    slot_count = (unit_count + devices - 1) // devices
    unit_ids = (
        jnp.arange(slot_count, dtype=jnp.int32)[None, :] * devices
        + jnp.arange(devices, dtype=jnp.int32)[:, None]
    )
    task_table = unit_ids // 2
    task_table = jnp.minimum(task_table, task_count - 1)
    tile_table = task_table % tile_count
    summed_parts = []
    for kind_index in range(3):
        term_fn = partial(row_term, grad_tiles, kind_index, stat_weight, mean_weight)
        summed_parts.append(
            lax.psum_scatter(
                term_fn(jnp.int32(0), lax.axis_size("dp") * row_share),
                "dp",
                scatter_dimension=0,
                tiled=True,
            )
        )
    totals = lax.psum((summed_parts[0], summed_parts[1], summed_parts[2]), "trial")
    pieces = jnp.stack(totals, 0).transpose(2, 0, 1, 3)
    group_tiles = lax.dynamic_slice_in_dim(tile_table, here_trial * data_n, data_n, 0).reshape(-1)
    outgoing = jnp.take(pieces, group_tiles, axis=0).reshape(
        data_n, slot_count, 3, row_share, block_order
    )
    received = lax.all_to_all(outgoing, "dp", split_axis=0, concat_axis=0, tiled=True)
    statistics = received.transpose(1, 2, 0, 3, 4).reshape(slot_count, 3, block_order, block_order)
    slot_tasks = lax.dynamic_index_in_dim(task_table, worker, 0, keepdims=False)
    slot_trial = slot_tasks // tile_count
    slot_power = exponents[slot_trial]
    slot_damping = dampings[slot_trial]
    average = statistics[:, 2]
    side_left = here_data % 2 == 0
    chosen = jnp.where(side_left, statistics[:, 0], statistics[:, 1])
    roots_now = jax.vmap(inverse_root)(chosen, slot_power, slot_damping)
    left_part = lax.cond(
        side_left, lambda: matmul_full(roots_now, average), lambda: jnp.zeros_like(average)
    )
    arrived = from_behind(left_part, "dp", 1)
    raw_update = lax.cond(
        side_left, lambda: jnp.zeros_like(average), lambda: matmul_full(arrived, roots_now)
    )
    finished = graft(raw_update, average).astype(jnp.bfloat16)
    outgoing_updates = finished.reshape(
        slot_count, data_n, row_share, trials_n, col_share
    ).transpose(3, 1, 0, 2, 4)
    returned = lax.all_to_all(
        lax.all_to_all(outgoing_updates, "trial", split_axis=0, concat_axis=0, tiled=True),
        "dp",
        split_axis=1,
        concat_axis=1,
        tiled=True,
    )
    flat_returned = returned.reshape(devices * slot_count, row_share, col_share)
    task_ids = jnp.arange(task_count, dtype=jnp.int32)
    holder_unit = 2 * task_ids + 1
    position = holder_unit % devices * slot_count + holder_unit // devices
    gathered = jnp.take(flat_returned, position, axis=0)
    return gathered.reshape(exponents.shape[0], tile_count, row_share, col_share)


def solution(mesh):
    placed = (P(("trial", "dp"), None, None, None), P(), P())
    return jax.shard_map(
        per_device,
        mesh=mesh,
        in_specs=placed,
        out_specs=P(None, None, "dp", "trial"),
        check_vma=False,
    )
```

profile of v0, /device:TPU:0, one launch (start us, length us, event | category | flops | bytes accessed | tf_op | source)
XLA Modules:
  0.0 645.4 jit_solution(5918245844691823995)
XLA Ops:
  6.5 3.2 copy.56
  9.8 3.4 multiply_bitcast_fusion.2
  13.2 3.4 multiply_bitcast_fusion.1
  16.6 3.6 multiply_bitcast_fusion
  20.2 5.5 copy.35
  25.7 5.4 copy.39
  31.2 0.6 copy-done.5
  31.8 0.6 dynamic-slice
  33.0 256.3 %all-reduce.8.cloned.1.call-done = (f32[512,4,512]{2,1,0:T(4,128)}, f32[512,4,512]{2,1,0:T(4,128)}, f32[512,4,512]{2,1,0:T(4,128)}) async-done(((f32[512,4,512]{2,1,0:T(4,128)}, f32[512,4,512]{2,1,0:T(4,128)}, f32[512,4,512]{2,1,0:T(4,128)}), (f32[512,4,512]{2,1,0:T(4,128)}, f32[512,4,512]{2,1,0:T(4,128)}, f32[512,4,512]{2,1,0:T(4,128)})) %all-reduce.8.cloned.1.call-update) | async-done | bytes 12582928
  289.3 1.3 constant_dynamic-slice_fusion
  290.6 1.0 copy.57
  291.6 1.0 copy.58
  292.5 1.1 constant_dynamic-slice_fusion.2
  293.6 1.0 copy.59
  294.8 61.4 %all-reduce.10.cloned.1.call-done = (f32[1,64,4,512]{3,1,0,2:T(8,128)}, f32[1,64,4,512]{3,1,0,2:T(8,128)}, f32[1,64,4,512]{3,1,0,2:T(8,128)}) async-done(((f32[1,64,4,512]{3,1,0,2:T(8,128)}, f32[1,64,4,512]{3,1,0,2:T(8,128)}, f32[1,64,4,512]{3,1,0,2:T(8,128)}), (f32[1,64,4,512]{3,1,0,2:T(8,128)}, f32[1,64,4,512]{3,1,0,2:T(8,128)}, f32[1,64,4,512]{3,1,0,2:T(8,128)})) %all-reduce.10.cloned.1.call-update) | async-done | bytes 1572880 | tf_op jit(solution)/shard_map/psum | solution.py:97
  356.2 1.6 maximum_bitcast_fusion
  357.8 3.6 gather_fusion.1
  361.4 6.8 %broadcast_select_fusion = f32[8,2,3,64,512]{4,3,2,1,0:T(8,128)} fusion(f32[8,2,3,64,512]{4,3,2,1,0:T(8,128)} %bitcast.61, pred[8,2]{1,0:T(8,128)(4,1)S(1)} %get-tuple-element.67), kind=kLoop, calls=%fused_computation.10 | loop fusion | flops 1572864 | bytes 12582928 | tf_op jit(solution)/shard_map/jit(_take)/select_n | solution.py:100
  368.2 5.1 all-to-all-start
  373.3 0.6 gather_fusion.2
  374.0 1.2 gather_fusion
  375.2 0.6 convert_element_type.39
  375.9 136.1 %all-to-all-done = f32[8,2,3,64,512]{4,3,2,1,0:T(8,128)} async-done(((f32[8,2,3,64,512]{4,3,2,1,0:T(8,128)}), f32[8,2,3,64,512]{4,3,2,1,0:T(8,128)}, u32[]{:S(2)}, u32[]{:S(2)}) %all-to-all-start) | async-done | bytes 6291488 | tf_op jit(solution)/shard_map/all_to_all | solution.py:103
  512.1 3.5 copy.42
  515.5 1.5 slice_bitcast_fusion
  517.1 1.3 multiply_reduce_fusion.2
  518.3 0.7 fusion.36
  520.1 15.8 %while.27 = (s32[2]{0:T(128)}, f32[2,512,512]{2,1,0:T(8,128)S(1)}, s32[2]{0:T(128)}, f32[2,512,512]{2,1,0:T(8,128)S(1)}) while((s32[2]{0:T(128)}, f32[2,512,512]{2,1,0:T(8,128)S(1)}, s32[2]{0:T(128)}, f32[2,512,512]{2,1,0:T(8,128)S(1)}) %tuple.37), condition=%region_8.10_spmd, body=%region_7.8_spmd | while | flops 3221749760 | bytes 10485837 | solution.py:32
  520.1 1.3 compare_reduce_fusion
  522.1 1.1 add_select_fusion
  523.4 3.6 convolution_select_fusion
  527.0 1.3 compare_reduce_fusion
  528.9 1.1 add_select_fusion
  530.2 3.6 convolution_select_fusion
  533.8 1.3 compare_reduce_fusion
  536.0 3.7 fusion.8
  539.7 3.6 fusion.6
  543.3 3.9 fusion.2
  547.2 6.7 %conditional.2 = (f32[2,512,512]{2,1,0:T(8,128)}) conditional(s32[]{:T(128)} %convert_element_type.38, () %tuple.21, (f32[2,512,512]{2,1,0:T(8,128)S(1)}, f32[2,512,512]{2,1,0:T(8,128)}) %tuple.23), branch_computations={%region_10.11_spmd, %region_11.12_spmd} | conditional | flops 3221225472 | bytes 6291464 | solution.py:113
  547.5 6.4 fusion.38
  553.9 1.4 collective-permute-start
  555.4 3.8 collective-permute-done
  560.8 19.3 %all_to_all.15 = bf16[4,8,2,64,128]{4,3,1,2,0:T(8,128)(2,1)S(1)} all-to-all(bf16[4,8,2,64,128]{4,3,1,2,0:T(8,128)(2,1)S(1)} %copy.43), channel_id=1, replica_groups=mesh['trial'=4,'dp'=8] {'trial'}, dimensions={0} | all-to-all | bytes 2097152 | tf_op jit(solution)/shard_map/all_to_all | solution.py:125
  580.1 1.9 copy.44
  581.9 28.1 %all-to-all-start.2 = ((bf16[4,8,2,64,128]{4,0,3,2,1:T(4,128)(2,1)}), bf16[4,8,2,64,128]{4,0,3,2,1:T(4,128)(2,1)S(1)}, u32[]{:S(2)}, u32[]{:S(2)}) async-start(bf16[4,8,2,64,128]{4,0,3,2,1:T(4,128)(2,1)} %copy.44), calls=%async_computation.2 | async-start | bytes 2097152 | tf_op jit(solution)/shard_map/all_to_all | solution.py:124
  610.1 26.5 %all-to-all-done.2 = bf16[4,8,2,64,128]{4,0,3,2,1:T(4,128)(2,1)S(1)} async-done(((bf16[4,8,2,64,128]{4,0,3,2,1:T(4,128)(2,1)}), bf16[4,8,2,64,128]{4,0,3,2,1:T(4,128)(2,1)S(1)}, u32[]{:S(2)}, u32[]{:S(2)}) %all-to-all-start.2) | async-done | bytes 1048608 | tf_op jit(solution)/shard_map/all_to_all | solution.py:124
  636.9 0.7 gather_fusion.3
  637.6 0.9 broadcast_select_fusion.1
  (40 shorter events, 4.0 us)
Async XLA Ops:
  6.5 366.8 %copy-start = (f32[8]{0:T(128)S(1)}, f32[8]{0:T(128)}, u32[]{:S(2)}) copy-start(f32[8]{0:T(128)} %param.11) | copy-start | bytes 100
  6.5 282.8 %all-reduce.8.cloned.1.call-start = ((), (), s32[]{:S(2)}) async-start(), calls=%async_computation.3 | async-start | bytes 25165824
  13.2 3.4 copy-start.4
  31.1 0.7 copy-start.5
  31.2 325.0 %all-reduce.10.cloned.1.call-start = ((), (), s32[]{:S(2)}) async-start(), calls=%async_computation.4 | async-start | bytes 3145728 | tf_op jit(solution)/shard_map/psum | solution.py:97
  368.2 5.8 copy-start.2
  368.2 143.9 %all-to-all-start = ((f32[8,2,3,64,512]{4,3,2,1,0:T(8,128)}), f32[8,2,3,64,512]{4,3,2,1,0:T(8,128)}, u32[]{:S(2)}, u32[]{:S(2)}) async-start(f32[8,2,3,64,512]{4,3,2,1,0:T(8,128)} %broadcast_select_fusion), calls=%async_computation | async-start | bytes 12582912 | tf_op jit(solution)/shard_map/all_to_all | solution.py:103
  553.9 5.3 collective-permute-start
  581.9 54.7 %all-to-all-start.2 = ((bf16[4,8,2,64,128]{4,0,3,2,1:T(4,128)(2,1)}), bf16[4,8,2,64,128]{4,0,3,2,1:T(4,128)(2,1)S(1)}, u32[]{:S(2)}, u32[]{:S(2)}) async-start(bf16[4,8,2,64,128]{4,0,3,2,1:T(4,128)(2,1)} %copy.44), calls=%async_computation.2 | async-start | bytes 2097152 | tf_op jit(solution)/shard_map/all_to_all | solution.py:124
  610.1 28.4 %copy-start.1 = (f32[8]{0:T(128)S(1)}, f32[8]{0:T(128)}, u32[]{:S(2)}) copy-start(f32[8]{0:T(128)} %param.11) | copy-start | bytes 100
Sparse Core Ops, SparseCore 0:
  31.3 258.0 all-reduce.7
  294.7 61.4 all-reduce.9
where the time goes:
time: 646 us; the launch traced here: 645 us
  waiting for transfers between devices  484 us (75%)
  local copies, waits for them, and re-layouts  35.6 us (6%)
  starting transfers between devices  34.7 us (5%)
  matrix products  31.7 us (5%)
  other arithmetic  23.1 us (4%)
  blocking collectives  19.3 us (3%)
  between operations  14.3 us (2%)
    unnamed x3, waiting for transfers between devices  256 us
    all_to_all x1, waiting for transfers between devices, per_device(): lax.all_to_all(outgoing, 'dp', split_axis=0, concat_axis=0, tiled=True)  136 us
    psum x1, waiting for transfers between devices, per_device(): lax.psum((summed_parts[0], summed_parts[1], summed_parts[2]), 'trial')  61.4 us
    all_to_all x1, starting transfers between devices, per_device(): lax.all_to_all(lax.all_to_all(outgoing_updates, 'trial', split_axis=0, co...  28.1 us
    all_to_all x1, waiting for transfers between devices, per_device(): lax.all_to_all(lax.all_to_all(outgoing_updates, 'trial', split_axis=0, co...  26.5 us
    dot_general x6, matrix products, matmul_full(): return jnp.matmul(first_mat, second_mat, precision=lax.Precision.HIGHEST)  24.9 us
    all_to_all x1, blocking collectives, per_device(): lax.all_to_all(outgoing_updates, 'trial', split_axis=0, concat_axis=0, ti...  19.3 us
  transfers between devices with their start and end apart: 5, of which 5 were waited for; matrix products, arithmetic and copies ran while one was open for 1% of the time, Pallas kernels for 0%

commit v1 on v0

v1 whole, which is shorter than its diff:
```python
import jax
import jax.numpy as jnp
from jax import lax
from jax.sharding import PartitionSpec as P


def matmul_full(first_mat, second_mat):
    return jnp.matmul(first_mat, second_mat, precision=lax.Precision.HIGHEST)


def inverse_root(statistic, exponent, damping):
    identity = jnp.eye(statistic.shape[-1], dtype=jnp.float32)
    shifted = statistic + damping * identity
    order_f = exponent.astype(jnp.float32)
    scaling = (1.0 + order_f) / (2.0 * jnp.sqrt(jnp.sum(shifted * shifted) + 1e-06))
    factor = ((order_f + 1.0) * identity - scaling * shifted) / order_f
    square = matmul_full(factor, factor)
    cube = matmul_full(square, factor)
    low = jnp.where(exponent == 2, factor, square)
    high = jnp.where(exponent == 2, square, cube)
    outer = jnp.where(exponent == 4, cube, square)
    tail = matmul_full(outer, order_f * high - (order_f + 1.0) * low)
    return jnp.exp(jnp.log(scaling) / order_f) / order_f * ((order_f + 1.0) * factor + tail)


def graft(raw_update, average):
    target = jnp.sqrt(jnp.mean(average * average))
    spread = jnp.sqrt(jnp.mean(raw_update * raw_update) + 1e-06)
    return raw_update * target / spread


def per_device(grads, exponents, dampings):
    trials_n = lax.axis_size("trial")
    data_n = lax.axis_size("dp")
    devices = trials_n * data_n
    settings = exponents.shape[0]
    block_order = grads.shape[-1]
    row_share = block_order // data_n
    col_share = block_order // trials_n
    here_data = lax.axis_index("dp")

    mine = lax.all_to_all(grads[0], "trial", split_axis=0, concat_axis=0, tiled=True)
    weight = 1.0 / (devices * block_order)
    left = jnp.einsum("irk,ick->rc", mine, mine, preferred_element_type=jnp.float32) * weight
    right = jnp.einsum("ikr,ikc->rc", mine, mine, preferred_element_type=jnp.float32) * weight
    average = jnp.sum(mine.astype(jnp.float32), axis=0) * (1.0 / devices)
    statistics, average = lax.psum((jnp.stack([left, right]), average), "dp")

    setting = here_data % settings
    roots = jax.vmap(inverse_root, in_axes=(0, None, None))(
        statistics, exponents[setting], dampings[setting]
    )
    raw_update = matmul_full(matmul_full(roots[0], average), roots[1])
    finished = graft(raw_update, average).astype(jnp.bfloat16)

    blocks = finished.reshape(data_n, row_share, trials_n, col_share).transpose(2, 0, 1, 3)
    returned = lax.all_to_all(
        blocks.reshape(devices, row_share, col_share),
        ("trial", "dp"),
        split_axis=0,
        concat_axis=0,
        tiled=True,
    )
    by_source = returned.reshape(trials_n, data_n, row_share, col_share)
    return by_source[:, :settings].transpose(1, 0, 2, 3)


def solution(mesh):
    placed = (P(("trial", "dp"), None, None, None), P(), P())
    return jax.shard_map(
        per_device,
        mesh=mesh,
        in_specs=placed,
        out_specs=P(None, None, "dp", "trial"),
        check_vma=False,
    )
```

time: 646 us -> 170 us (0.26)
  waiting for transfers between devices: 484 us -> 72.6 us
  starting transfers between devices: 34.7 us -> 0.01 us
  local copies, waits for them, and re-layouts: 35.6 us -> 2.96 us
  blocking collectives: 19.3 us -> 51.2 us
  other arithmetic: 23.1 us -> 7.56 us
  matrix products: 31.7 us -> 18.3 us
    unnamed x3 -> x1, waiting for transfers between devices: 256 us -> 0.02 us
    all_to_all x2 -> x0, waiting for transfers between devices: 163 us -> none  [the longest x1 136 us: per_device(): lax.all_to_all(outgoing, 'dp', split_axis=0, concat_axis=0, tiled=True)]
    all_to_all x2 -> x0, starting transfers between devices: 33.2 us -> none  [the longest x1 28.1 us: per_device(): lax.all_to_all(lax.all_to_all(outgoing_updates, 'trial', split_axis=0, co...]
    all_to_all x1 -> x2, blocking collectives: 19.3 us -> 51.2 us  [the longest x1 30.5 us: per_device(): lax.all_to_all(grads[0], 'trial', split_axis=0, concat_axis=0, tiled=True)]
    psum x1, waiting for transfers between devices: 61.4 us -> 72.6 us  [per_device(): statistics, average = lax.psum((jnp.stack([left, right]), average), 'dp')]
    mul x2 -> x0, local copies, waits for them, and re-layouts: 10.9 us -> none  [the longest x1 5.47 us: row_term(): jnp.einsum('nrk,nck->rnc', band, grad_tiles, preferred_element_type=jnp.f...]
    dot_general x6 -> x5, matrix products: 24.9 us -> 15.7 us  [matmul_full(): return jnp.matmul(first_mat, second_mat, precision=lax.Precision.HIGHEST)]
    select_n x5 -> x0, other arithmetic: 7.78 us -> none  [the longest x2 6.83 us: per_device(): jnp.take(pieces, group_tiles, axis=0)]
  transfers between devices with their start and end apart: 5 -> 1, of which waited for: 5 -> 1; matrix products, arithmetic and copies ran while one was open for 1% -> 1% of each run, Pallas kernels for 0% -> 0%
where the time goes in v1:
time: 170 us; the launch traced here: 169 us
  waiting for transfers between devices  72.6 us (43%)
  blocking collectives  51.2 us (30%)
  matrix products  18.3 us (11%)
  between operations  16.9 us (10%)
  other arithmetic  7.56 us (4%)
  local copies, waits for them, and re-layouts  2.96 us (2%)
    psum x1, waiting for transfers between devices, per_device(): statistics, average = lax.psum((jnp.stack([left, right]), average), 'dp')  72.6 us
    all_to_all x1, blocking collectives, per_device(): lax.all_to_all(grads[0], 'trial', split_axis=0, concat_axis=0, tiled=True)  30.5 us
    all_to_all x1, blocking collectives, per_device(): lax.all_to_all(blocks.reshape(devices, row_share, col_share), ('trial', '...  20.6 us
    dot_general x5, matrix products, matmul_full(): return jnp.matmul(first_mat, second_mat, precision=lax.Precision.HIGHEST)  15.7 us
  transfers between devices with their start and end apart: 1, of which 1 were waited for; matrix products, arithmetic and copies ran while one was open for 1% of the time, Pallas kernels for 0%

profile of v1, /device:TPU:0, one launch (start us, length us, event | category | flops | bytes accessed | tf_op | source)
XLA Modules:
  0.0 169.5 jit_solution(659411991829953940)
XLA Ops:
  6.5 0.0 all-reduce.3.cloned.1.call-start
  6.5 30.5 %all_to_all.10 = bf16[4,512,512]{2,1,0:T(8,128)(2,1)S(1)} all-to-all(bf16[4,512,512]{2,1,0:T(8,128)(2,1)} %bitcast.45), channel_id=1, replica_groups=mesh['trial'=4,'dp'=8] {'trial'}, dimensions={0} | all-to-all | bytes 4194304 | tf_op jit(solution)/shard_map/all_to_all | solution.py:42
  37.1 0.3 convert_reduce_fusion
  37.4 1.1 broadcast_multiply_fusion
  38.5 1.3 fusion.12
  39.8 1.3 fusion.14
  41.1 1.5 pad_maximum_fusion
  42.5 0.0 copy-start.2
  42.5 0.0 copy-start.3
  42.5 0.0 all-reduce.3.cloned.1.call-update
  42.6 0.6 copy-done.2
  43.2 0.6 dynamic_slice.6
  44.4 0.0 copy-done.3
  44.4 0.6 dynamic_slice.7
  46.4 0.9 fusion.19
  47.2 72.6 %all-reduce.3.cloned.1.call-done = (f32[512,512]{1,0:T(8,128)}, f32[2,512,512]{2,1,0:T(8,128)}) async-done(((f32[512,512]{1,0:T(8,128)}, f32[2,512,512]{2,1,0:T(8,128)}), (f32[512,512]{1,0:T(8,128)}, f32[2,512,512]{2,1,0:T(8,128)})) %all-reduce.3.cloned.1.call-update) | async-done | bytes 3145744 | tf_op jit(solution)/shard_map/psum | solution.py:47
  119.8 0.0 copy-start
  119.8 2.1 %multiply_reduce_fusion = f32[2]{0:T(128)S(1)} fusion(f32[2,512,512]{2,1,0:T(8,128)} %get-tuple-element.6, f32[512,512]{1,0:T(8,128)S(1)} %get-tuple-element.12), kind=kLoop, calls=%fused_computation.11 | loop fusion | flops 1572862 | bytes 3145736 | tf_op jit(solution)/shard_map/vmap()/reduce_sum | solution.py:15
  122.0 0.1 copy-done
  122.1 0.6 subtract_divide_fusion
  122.6 3.5 %fusion.23 = f32[2,512,512]{2,1,0:T(8,128)S(1)} fusion(f32[2,512,512]{2,1,0:T(8,128)S(1)} %subtract_divide_fusion), kind=kOutput, calls=%fused_computation.35 | convolution fusion | flops 3221225472 | bytes 4194304 | tf_op jit(solution)/shard_map/vmap()/dot_general | solution.py:8
  126.2 0.0 copy-start.1
  126.2 3.5 %fusion.24 = f32[2,512,512]{2,1,0:T(8,128)S(1)} fusion(f32[2,512,512]{2,1,0:T(8,128)S(1)} %fusion.23, f32[2,512,512]{2,1,0:T(8,128)S(1)} %subtract_divide_fusion), kind=kOutput, calls=%fused_computation.36 | convolution fusion | flops 3221225472 | bytes 6291456 | tf_op jit(solution)/shard_map/vmap()/dot_general | solution.py:8
  129.7 0.0 copy-done.1
  129.7 0.9 multiply_reduce_fusion.2
  130.7 4.2 %add_multiply_fusion = f32[2,512,512]{2,1,0:T(8,128)S(1)} fusion(f32[2,512,512]{2,1,0:T(8,128)S(1)} %subtract_divide_fusion, f32[2,512,512]{2,1,0:T(8,128)S(1)} %fusion.23, f32[2,512,512]{2,1,0:T(8,128)S(1)} %fusion.24, f32[]{:T(128)} %bitcast, f32[]{:T(128)S(6)} %add.44, f32[2]{0:T(128)S(1)} %get-tuple-element.7, pred[]{:T(512)} %bitcast.8, pred[]{:T(512)} %bitcast.7), kind=kOutput, calls=%fused_computation.2 | convolution fusion | flops 3225944064 | bytes 8388626 | tf_op jit(solution)/shard_map/vmap()/dot_general | solution.py:8
  134.9 1.9 %fusion.16 = f32[512,512]{1,0:T(8,128)S(1)} fusion(f32[512,512]{1,0:T(8,128)S(1)} %copy-done.1, f32[2,512,512]{2,1,0:T(8,128)S(1)} %add_multiply_fusion), kind=kOutput, calls=%fused_computation.21 | convolution fusion | flops 1610612736 | bytes 3145728 | tf_op jit(solution)/shard_map/dot_general | solution.py:8
  136.8 2.6 %multiply_reduce_fusion.1 = (f32[]{:T(128)}, f32[512,512]{1,0:T(8,128)S(1)}) fusion(f32[512,512]{1,0:T(8,128)S(1)} %fusion.16, f32[2,512,512]{2,1,0:T(8,128)S(1)} %add_multiply_fusion), kind=kOutput, calls=%fused_computation.23 | convolution fusion | flops 1611137024 | bytes 3145732 | tf_op jit(solution)/shard_map/dot_general | solution.py:8
  140.8 0.1 divide_convert_fusion
  140.9 0.1 reshape.39
  141.0 0.1 copy.9
  141.2 20.6 %all_to_all.11 = bf16[32,64,128]{2,1,0:T(8,128)(2,1)S(1)} all-to-all(bf16[32,64,128]{2,1,0:T(8,128)(2,1)S(1)} %bitcast.46), channel_id=1, replica_groups=mesh['trial'=4,'dp'=8] {'trial','dp'}, dimensions={0} | all-to-all | bytes 1048576 | tf_op jit(solution)/shard_map/all_to_all | solution.py:57
  161.8 0.8 copy.10
  (1 shorter events, 0.0 us)
Async XLA Ops:
  6.5 113.3 %all-reduce.3.cloned.1.call-start = ((), (), s32[]{:S(2)}) async-start(), calls=%async_computation.2 | async-start | bytes 6291456 | tf_op jit(solution)/shard_map/psum | solution.py:47
  42.5 0.7 copy-start.2
  42.5 1.9 %copy-start.3 = (f32[8]{0:T(128)S(1)}, f32[8]{0:T(128)}, u32[]{:S(2)}) copy-start(f32[8]{0:T(128)} %param.5) | copy-start | bytes 100
  119.8 2.2 %copy-start = (f32[2,512,512]{2,1,0:T(8,128)S(1)}, f32[2,512,512]{2,1,0:T(8,128)}, u32[]{:S(2)}) copy-start(f32[2,512,512]{2,1,0:T(8,128)} %get-tuple-element.6) | copy-start | bytes 6291460
  126.2 3.6 %copy-start.1 = (f32[512,512]{1,0:T(8,128)S(1)}, f32[512,512]{1,0:T(8,128)}, u32[]{:S(2)}) copy-start(f32[512,512]{1,0:T(8,128)} %get-tuple-element.5) | copy-start | bytes 3145732
Sparse Core Ops, SparseCore 0:
  42.7 77.1 all-reduce.2

commit v2 on v1

v2 whole, which is shorter than its diff:
```python
import functools

import jax
import jax.numpy as jnp
from jax import lax
from jax.experimental import pallas as pl
from jax.experimental.pallas import tpu as pltpu
from jax.sharding import PartitionSpec as P

MESH = pl.DeviceIdType.MESH
BANDS = 4
CHUNKS = 6
F32 = jnp.float32
BF16 = jnp.bfloat16


def stat_pieces(order):
    band = order // BANDS
    pieces = []
    for kind in range(2):
        base = kind * 2 * band
        pieces.append((kind, 3, base, 0))
        pieces.append((kind, 2, base + band, 0))
        pieces.append((kind, 0, base + band, 3 * band))
        pieces.append((kind, 1, 4 * band, kind * 2 * band))
    return band, pieces


def packed_rows(order):
    return 5 * (order // BANDS) + order


def add_tile(part, tile, first):
    order = part.shape[1]
    band, pieces = stat_pieces(order)
    for kind, index, row, col in pieces:
        width = (index + 1) * band
        if kind == 0:
            term = lax.dot_general(
                tile[index * band : (index + 1) * band, :],
                tile[0:width, :],
                (((1,), (1,)), ((), ())),
                preferred_element_type=F32,
            )
        else:
            term = lax.dot_general(
                tile[:, index * band : (index + 1) * band],
                tile[:, 0:width],
                (((0,), (0,)), ((), ())),
                preferred_element_type=F32,
            )
        place = (slice(row, row + band), slice(col, col + width))
        part[place] = term if first else part[place] + term
    place = (slice(5 * band, 5 * band + order), slice(0, order))
    term = tile[...].astype(F32)
    part[place] = term if first else part[place] + term


def sum_kernel(
    trials_n, data_n, chunks, grads, total, mine, part, swap, passed, outgoing,
    grad_send, grad_recv, swap_send, swap_recv, pass_send, pass_recv,
    back_send, back_recv, share_send, share_recv,
):
    here_t = lax.axis_index("trial")
    here_d = lax.axis_index("dp")
    chips = data_n // 2
    core = lax.rem(here_d, 2)
    chip = here_d // 2
    partner = here_d + 1 - 2 * core
    rows = part.shape[0]
    half = rows // 2
    size = half // (2 * chunks)

    barrier = pltpu.get_barrier_semaphore()
    for step in range(1, trials_n):
        peer = lax.rem(here_t + step, trials_n)
        pl.semaphore_signal(barrier, inc=1, device_id=(peer, here_d), device_id_type=MESH)
    pl.semaphore_signal(barrier, inc=1, device_id=(here_t, partner), device_id_type=MESH)

    @pl.when(chip > 0)
    def _():
        pl.semaphore_signal(barrier, inc=1, device_id=(here_t, here_d - 2), device_id_type=MESH)

    @pl.when(chip < chips - 1)
    def _():
        pl.semaphore_signal(barrier, inc=1, device_id=(here_t, here_d + 2), device_id_type=MESH)

    neighbours = jnp.where(chip > 0, 1, 0) + jnp.where(chip < chips - 1, 1, 0)
    pl.semaphore_wait(barrier, trials_n + neighbours)

    def grad_copy(step):
        peer = lax.rem(here_t + step, trials_n)
        return pltpu.make_async_remote_copy(
            src_ref=grads.at[peer],
            dst_ref=mine.at[step - 1],
            send_sem=grad_send.at[step - 1],
            recv_sem=grad_recv.at[step - 1],
            device_id=(peer, here_d),
            device_id_type=MESH,
        )

    for step in range(1, trials_n):
        grad_copy(step).start()
    add_tile(part, grads.at[here_t], True)
    for step in range(1, trials_n):
        grad_copy(step).wait_recv()
        add_tile(part, mine.at[step - 1], False)

    def chunk_at(owner, way, k):
        return pl.ds(pl.multiple_of(owner * half + (way * chunks + k) * size, 8), size)

    def swap_copy(way, k):
        return pltpu.make_async_remote_copy(
            src_ref=part.at[chunk_at(1 - core, way, k)],
            dst_ref=swap.at[way, k],
            send_sem=swap_send.at[way, k],
            recv_sem=swap_recv.at[way, k],
            device_id=(here_t, partner),
            device_id_type=MESH,
        )

    def pass_copy(way, k):
        return pltpu.make_async_remote_copy(
            src_ref=outgoing.at[way, k],
            dst_ref=passed.at[way, k],
            send_sem=pass_send.at[way, k],
            recv_sem=pass_recv.at[way, k],
            device_id=(here_t, here_d + 2 - 4 * way),
            device_id_type=MESH,
        )

    def back_copy(way, k):
        return pltpu.make_async_remote_copy(
            src_ref=total.at[chunk_at(core, way, k)],
            dst_ref=total.at[chunk_at(core, way, k)],
            send_sem=back_send.at[way, k],
            recv_sem=back_recv.at[way, k],
            device_id=(here_t, here_d - 2 + 4 * way),
            device_id_type=MESH,
        )

    def share_copy(way, k):
        return pltpu.make_async_remote_copy(
            src_ref=total.at[chunk_at(core, way, k)],
            dst_ref=total.at[chunk_at(core, way, k)],
            send_sem=share_send.at[way, k],
            recv_sem=share_recv.at[way, k],
            device_id=(here_t, partner),
            device_id_type=MESH,
        )

    def shared_by_partner(way, k):
        return pltpu.make_async_remote_copy(
            src_ref=total.at[chunk_at(1 - core, way, k)],
            dst_ref=total.at[chunk_at(1 - core, way, k)],
            send_sem=share_send.at[way, k],
            recv_sem=share_recv.at[way, k],
            device_id=(here_t, partner),
            device_id_type=MESH,
        )

    order = [(way, k) for k in range(chunks) for way in range(2)]
    is_start = (chip == 0, chip == chips - 1)
    is_end = (chip == chips - 1, chip == 0)

    for way, k in order:
        swap_copy(way, k).start()
    for way, k in order:
        swap_copy(way, k).wait_recv()
        outgoing[way, k] = part[chunk_at(core, way, k), :] + swap[way, k]

        @pl.when(jnp.logical_not(is_start[way]))
        def _():
            pass_copy(way, k).wait_recv()
            outgoing[way, k] = outgoing[way, k] + passed[way, k]

        @pl.when(jnp.logical_not(is_end[way]))
        def _():
            pass_copy(way, k).start()

        @pl.when(is_end[way])
        def _():
            total[chunk_at(core, way, k), :] = outgoing[way, k]
            back_copy(way, k).start()
            share_copy(way, k).start()

    for way, k in order:

        @pl.when(jnp.logical_not(is_end[way]))
        def _():
            back_copy(way, k).wait_recv()

            @pl.when(jnp.logical_not(is_start[way]))
            def _():
                back_copy(way, k).start()

            share_copy(way, k).start()

    for way, k in order:
        shared_by_partner(way, k).wait_recv()
    for way, k in order:
        swap_copy(way, k).wait_send()
        share_copy(way, k).wait_send()

        @pl.when(jnp.logical_not(is_end[way]))
        def _():
            pass_copy(way, k).wait_send()

        @pl.when(jnp.logical_not(is_start[way]))
        def _():
            back_copy(way, k).wait_send()

    for step in range(1, trials_n):
        grad_copy(step).wait_send()


def split(value):
    high = value.astype(BF16)
    return high, (value - high.astype(F32)).astype(BF16)


def product(first, second):
    def dot(a, b):
        return jnp.dot(a, b, preferred_element_type=F32)

    return dot(first[0], second[0]) + (dot(first[0], second[1]) + dot(first[1], second[0]))


def update_kernel(
    trials_n, data_n, settings, packed, exponents, dampings, out,
    stat, factor, square, cube, root_high, root_low, finished, own_sem, send_sem, recv_sem,
):
    here_t = lax.axis_index("trial")
    here_d = lax.axis_index("dp")
    devices = trials_n * data_n
    here = here_t * data_n + here_d
    order = packed.shape[1]
    setting = lax.rem(here_d, settings)

    barrier = pltpu.get_barrier_semaphore()

    @pl.loop(1, devices)
    def _(step):
        peer = lax.rem(here + step, devices)
        pl.semaphore_signal(
            barrier, inc=1, device_id=(peer // data_n, lax.rem(peer, data_n)), device_id_type=MESH
        )

    band, pieces = stat_pieces(order)
    exponent = jnp.full((1, 1), exponents[setting], jnp.int32)
    damping = jnp.full((1, 1), dampings[setting], F32)
    order_f = exponent.astype(F32)
    eye = (
        lax.broadcasted_iota(jnp.int32, (order, order), 0)
        == lax.broadcasted_iota(jnp.int32, (order, order), 1)
    )
    weight = 1.0 / (devices * order)

    for kind in range(2):
        for piece_kind, index, row, col in pieces:
            if piece_kind != kind:
                continue
            for other in range(index + 1):
                block = packed[row : row + band, col + other * band : col + (other + 1) * band]
                block = block * weight
                stat[index * band : (index + 1) * band, other * band : (other + 1) * band] = block
                if other < index:
                    stat[other * band : (other + 1) * band, index * band : (index + 1) * band] = (
                        block.T
                    )
        shifted = stat[...] + jnp.where(eye, damping, 0.0)
        norm = jnp.sqrt(jnp.sum(shifted * shifted, keepdims=True) + 1e-06)
        scaling = (1.0 + order_f) / (2.0 * norm)
        factor[...] = (jnp.where(eye, order_f + 1.0, 0.0) - scaling * shifted) / order_f
        factor_parts = split(factor[...])
        square[...] = product(factor_parts, factor_parts)
        square_parts = split(square[...])
        cube[...] = product(square_parts, factor_parts)
        low = jnp.where(exponent == 2, factor[...], square[...])
        high = jnp.where(exponent == 2, square[...], cube[...])
        outer = jnp.where(exponent == 4, cube[...], square[...])
        tail = product(split(outer), split(order_f * high - (order_f + 1.0) * low))
        root = (jnp.exp(jnp.log(scaling) / order_f) / order_f) * (
            (order_f + 1.0) * factor[...] + tail
        )
        root_high[kind], root_low[kind] = split(root)

    average = packed[5 * band : 5 * band + order, :] * (1.0 / devices)
    middle = product((root_high[0], root_low[0]), split(average))
    raw = product(split(middle), (root_high[1], root_low[1]))
    count = order * order
    target = jnp.sqrt(jnp.sum(average * average, keepdims=True) / count)
    spread = jnp.sqrt(jnp.sum(raw * raw, keepdims=True) / count + 1e-06)
    stat[...] = raw * target / spread
    row_share, col_share = out.shape[2:]
    for t in range(trials_n):
        for d in range(data_n):
            finished[t, d] = stat[
                d * row_share : (d + 1) * row_share, t * col_share : (t + 1) * col_share
            ].astype(BF16)

    pl.semaphore_wait(barrier, devices - 1)

    def block_copy(peer):
        peer_t, peer_d = peer // data_n, lax.rem(peer, data_n)
        return pltpu.make_async_remote_copy(
            src_ref=finished.at[peer_t, peer_d],
            dst_ref=out.at[here_d, here_t],
            send_sem=send_sem.at[peer],
            recv_sem=recv_sem.at[here_d, here_t],
            device_id=(peer_t, peer_d),
            device_id_type=MESH,
        )

    own = pltpu.make_async_copy(finished.at[here_t, here_d], out.at[setting, here_t], own_sem)

    @pl.when(here_d < settings)
    def _():
        own.start()

        @pl.loop(1, devices)
        def _(step):
            block_copy(lax.rem(here + step, devices)).start()

    @pl.loop(0, settings * trials_n)
    def _(source):
        source_t, source_d = source // settings, lax.rem(source, settings)

        @pl.when(source_t * data_n + source_d != here)
        def _():
            pltpu.make_async_remote_copy(
                src_ref=finished.at[here_t, here_d],
                dst_ref=out.at[source_d, source_t],
                send_sem=send_sem.at[here],
                recv_sem=recv_sem.at[source_d, source_t],
                device_id=(source_t, source_d),
                device_id_type=MESH,
            ).wait_recv()

    @pl.when(here_d < settings)
    def _():
        own.wait()

        @pl.loop(1, devices)
        def _(step):
            block_copy(lax.rem(here + step, devices)).wait_send()


def per_device(grads, exponents, dampings):
    trials_n = lax.axis_size("trial")
    data_n = lax.axis_size("dp")
    devices = trials_n * data_n
    settings = exponents.shape[0]
    tiles, order = grads.shape[1], grads.shape[-1]
    assert tiles == trials_n and data_n >= settings and data_n % 2 == 0
    rows = packed_rows(order)
    size = rows // (4 * CHUNKS)
    in_vmem = pl.BlockSpec(memory_space=pltpu.VMEM)
    in_smem = pl.BlockSpec(memory_space=pltpu.SMEM)
    dma = pltpu.SemaphoreType.DMA
    pairs = dma((2, CHUNKS))

    packed = pl.pallas_call(
        functools.partial(sum_kernel, trials_n, data_n, CHUNKS),
        out_shape=jax.ShapeDtypeStruct((rows, order), F32),
        in_specs=[in_vmem],
        out_specs=in_vmem,
        scratch_shapes=[
            pltpu.VMEM((trials_n - 1, order, order), BF16),
            pltpu.VMEM((rows, order), F32),
            pltpu.VMEM((2, CHUNKS, size, order), F32),
            pltpu.VMEM((2, CHUNKS, size, order), F32),
            pltpu.VMEM((2, CHUNKS, size, order), F32),
            dma((trials_n - 1,)),
            dma((trials_n - 1,)),
        ]
        + [pairs] * 8,
        compiler_params=pltpu.CompilerParams(
            collective_id=0, has_side_effects=True, vmem_limit_bytes=40 * 1024 * 1024
        ),
    )(grads[0])

    out = pl.pallas_call(
        functools.partial(update_kernel, trials_n, data_n, settings),
        out_shape=jax.ShapeDtypeStruct(
            (settings, tiles, order // data_n, order // trials_n), BF16
        ),
        in_specs=[in_vmem, in_smem, in_smem],
        out_specs=in_vmem,
        scratch_shapes=[
            pltpu.VMEM((order, order), F32),
            pltpu.VMEM((order, order), F32),
            pltpu.VMEM((order, order), F32),
            pltpu.VMEM((order, order), F32),
            pltpu.VMEM((2, order, order), BF16),
            pltpu.VMEM((2, order, order), BF16),
            pltpu.VMEM((trials_n, data_n, order // data_n, order // trials_n), BF16),
            dma,
            dma((devices,)),
            dma((settings, trials_n)),
        ],
        compiler_params=pltpu.CompilerParams(
            collective_id=1, has_side_effects=True, vmem_limit_bytes=40 * 1024 * 1024
        ),
    )(packed, exponents, dampings)
    return out


def solution(mesh):
    placed = (P(("trial", "dp"), None, None, None), P(), P())
    return jax.shard_map(
        per_device,
        mesh=mesh,
        in_specs=placed,
        out_specs=P(None, None, "dp", "trial"),
        check_vma=False,
    )
```

time: 170 us -> 244 us (1.44)
  Pallas kernels: 0 us -> 241 us
  waiting for transfers between devices: 72.6 us -> 0 us
  blocking collectives: 51.2 us -> 0 us
  matrix products: 18.3 us -> 0 us
  between operations: 16.9 us -> 0.03 us
  other arithmetic: 7.56 us -> 0 us
    pallas_call x0 -> x2, Pallas kernels: none -> 241 us  [the longest x1 217 us: per_device(): pl.pallas_call(functools.partial(sum_kernel, trials_n, data_n, CHUNKS), o...]
    psum x1 -> x0, waiting for transfers between devices: 72.6 us -> none  [per_device(): statistics, average = lax.psum((jnp.stack([left, right]), average), 'dp')]
    all_to_all x2 -> x0, blocking collectives: 51.2 us -> none  [the longest x1 30.5 us: per_device(): lax.all_to_all(grads[0], 'trial', split_axis=0, concat_axis=0, tiled=True)]
    dot_general x7 -> x0, matrix products: 18.3 us -> none  [the longest x5 15.7 us: matmul_full(): return jnp.matmul(first_mat, second_mat, precision=lax.Precision.HIGHEST)]
    reduce_sum x3 -> x0, other arithmetic: 3.4 us -> none  [the longest x1 2.13 us: inverse_root(): jnp.sum(shifted * shifted) + 1e-06]
  transfers between devices with their start and end apart: 1 -> 0, of which waited for: 1 -> 0; matrix products, arithmetic and copies ran while one was open for 1% -> 0% of each run, Pallas kernels for 0% -> 0%
where the time goes in v2:
time: 244 us
  Pallas kernels  241 us (99%)
    pallas_call x1, Pallas kernels, per_device(): pl.pallas_call(functools.partial(sum_kernel, trials_n, data_n, CHUNKS), o...  217 us
    pallas_call x1, Pallas kernels, per_device(): pl.pallas_call(functools.partial(update_kernel, trials_n, data_n, setting...  24.7 us

profile of v2, /device:TPU:0, one launch (start us, length us, event | category | flops | bytes accessed | tf_op | source)
XLA Modules:
  0.0 243.8 jit_solution(11460999776428274071)
XLA Ops:
  0.0 0.0 copy-start.2
  0.0 0.0 copy-start.1
  0.0 0.0 copy-start
  0.0 1.6 copy-done
  1.6 216.7 %shard_map.37.packed = f32[1152,512]{1,0:T(8,128)S(1)} custom-call(bf16[4,512,512]{2,1,0:T(8,128)(2,1)S(1)} %bitcast.1), custom_call_target="tpu_custom_call" | custom-call | tf_op jit(solution)/shard_map/pallas_call | solution.py:363
  218.3 0.0 copy-done.2
  218.4 0.0 copy-done.1
  218.4 24.7 %shard_map.38 = bf16[8,4,64,128]{3,2,1,0:T(8,128)(2,1)S(1)} custom-call(f32[1152,512]{1,0:T(8,128)S(1)} %shard_map.37.packed, s32[8]{0:T(128)S(1)} %copy-done.1, f32[8]{0:T(128)S(1)} %copy-done.2), custom_call_target="tpu_custom_call" | custom-call | tf_op jit(solution)/shard_map/pallas_call | solution.py:383
  243.0 0.8 copy.5
Async XLA Ops:
  0.0 218.3 %copy-start.2 = (f32[8]{0:T(128)S(1)}, f32[8]{0:T(128)}, u32[]{:S(2)}) copy-start(f32[8]{0:T(128)} %dampings.1) | copy-start | bytes 100
  0.0 218.4 %copy-start.1 = (s32[8]{0:T(128)S(1)}, s32[8]{0:T(128)}, u32[]{:S(2)}) copy-start(s32[8]{0:T(128)} %exponents.1) | copy-start | bytes 100
  0.0 1.6 copy-start

commit v3 on v2

--- a/solution.py
+++ b/solution.py
@@ -9,7 +9,7 @@
 
 MESH = pl.DeviceIdType.MESH
 BANDS = 4
-CHUNKS = 6
+CHUNKS = 3
 F32 = jnp.float32
 BF16 = jnp.bfloat16
 
@@ -165,7 +165,10 @@
 
     for way, k in order:
         swap_copy(way, k).start()
-    for way, k in order:
+    last = chips - 1
+    distance = (chip, last - chip)
+
+    def reduce_chunk(way, k):
         swap_copy(way, k).wait_recv()
         outgoing[way, k] = part[chunk_at(core, way, k), :] + swap[way, k]
 
@@ -184,17 +187,30 @@
             back_copy(way, k).start()
             share_copy(way, k).start()
 
-    for way, k in order:
-
-        @pl.when(jnp.logical_not(is_end[way]))
-        def _():
-            back_copy(way, k).wait_recv()
-
-            @pl.when(jnp.logical_not(is_start[way]))
+    def return_chunk(way, k):
+        back_copy(way, k).wait_recv()
+
+        @pl.when(jnp.logical_not(is_start[way]))
+        def _():
+            back_copy(way, k).start()
+
+        share_copy(way, k).start()
+
+    @pl.loop(0, chunks + 2 * last)
+    def _(step):
+        for way in range(2):
+            k = step - distance[way]
+
+            @pl.when((k >= 0) & (k < chunks))
             def _():
-                back_copy(way, k).start()
-
-            share_copy(way, k).start()
+                reduce_chunk(way, k)
+
+        for way in range(2):
+            k = step - last - distance[1 - way]
+
+            @pl.when((k >= 0) & (k < chunks) & jnp.logical_not(is_end[way]))
+            def _():
+                return_chunk(way, k)
 
     for way, k in order:
         shared_by_partner(way, k).wait_recv()

time: 244 us -> 99.6 us (0.41)
  Pallas kernels: 241 us -> 97 us
    pallas_call x1, Pallas kernels: 217 us -> 75 us  [per_device(): pl.pallas_call(functools.partial(sum_kernel, trials_n, data_n, CHUNKS), o...]
    pallas_call x1, Pallas kernels: 24.7 us -> 22 us  [per_device(): pl.pallas_call(functools.partial(update_kernel, trials_n, data_n, setting...]
where the time goes in v3:
time: 99.6 us; the launch traced here: 99.4 us
  Pallas kernels  97 us (97%)
  local copies, waits for them, and re-layouts  2.42 us (2%)
    pallas_call x1, Pallas kernels, per_device(): pl.pallas_call(functools.partial(sum_kernel, trials_n, data_n, CHUNKS), o...  75 us
    pallas_call x1, Pallas kernels, per_device(): pl.pallas_call(functools.partial(update_kernel, trials_n, data_n, setting...  22 us
    unnamed x7, local copies, waits for them, and re-layouts  2.42 us

profile of v3, /device:TPU:0, one launch (start us, length us, event | category | flops | bytes accessed | tf_op | source)
XLA Modules:
  0.0 99.4 jit_solution(3888941867318271898)
XLA Ops:
  0.0 0.0 copy-start.2
  0.0 0.0 copy-start.1
  0.0 0.0 copy-start
  0.0 1.6 %copy-done = bf16[1,4,512,512]{3,2,1,0:T(8,128)(2,1)S(1)} copy-done((bf16[1,4,512,512]{3,2,1,0:T(8,128)(2,1)S(1)}, bf16[1,4,512,512]{3,2,1,0:T(8,128)(2,1)}, u32[]{:S(2)}) %copy-start) | copy-done | bytes 2097176
  1.6 75.0 %shard_map.37.packed = f32[1152,512]{1,0:T(8,128)S(1)} custom-call(bf16[4,512,512]{2,1,0:T(8,128)(2,1)S(1)} %bitcast.1), custom_call_target="tpu_custom_call" | custom-call | tf_op jit(solution)/shard_map/pallas_call | solution.py:379
  76.6 0.0 copy-done.2
  76.6 0.0 copy-done.1
  76.7 22.0 %shard_map.38 = bf16[8,4,64,128]{3,2,1,0:T(8,128)(2,1)S(1)} custom-call(f32[1152,512]{1,0:T(8,128)S(1)} %shard_map.37.packed, s32[8]{0:T(128)S(1)} %copy-done.1, f32[8]{0:T(128)S(1)} %copy-done.2), custom_call_target="tpu_custom_call" | custom-call | tf_op jit(solution)/shard_map/pallas_call | solution.py:399
  98.6 0.8 copy.5
Async XLA Ops:
  0.0 76.6 %copy-start.2 = (f32[8]{0:T(128)S(1)}, f32[8]{0:T(128)}, u32[]{:S(2)}) copy-start(f32[8]{0:T(128)} %dampings.1) | copy-start | bytes 100
  0.0 76.6 %copy-start.1 = (s32[8]{0:T(128)S(1)}, s32[8]{0:T(128)}, u32[]{:S(2)}) copy-start(s32[8]{0:T(128)} %exponents.1) | copy-start | bytes 100
  0.0 1.6 %copy-start = (bf16[1,4,512,512]{3,2,1,0:T(8,128)(2,1)S(1)}, bf16[1,4,512,512]{3,2,1,0:T(8,128)(2,1)}, u32[]{:S(2)}) copy-start(bf16[1,4,512,512]{3,2,1,0:T(8,128)(2,1)} %param.3) | copy-start | bytes 6291460

commit v4 on v3

--- a/solution.py
+++ b/solution.py
@@ -9,51 +9,68 @@
 
 MESH = pl.DeviceIdType.MESH
 BANDS = 4
-CHUNKS = 3
 F32 = jnp.float32
 BF16 = jnp.bfloat16
 
 
 def stat_pieces(order):
     band = order // BANDS
-    pieces = []
-    for kind in range(2):
-        base = kind * 2 * band
-        pieces.append((kind, 3, base, 0))
-        pieces.append((kind, 2, base + band, 0))
-        pieces.append((kind, 0, base + band, 3 * band))
-        pieces.append((kind, 1, 4 * band, kind * 2 * band))
-    return band, pieces
-
-
-def packed_rows(order):
-    return 5 * (order // BANDS) + order
-
-
-def add_tile(part, tile, first):
+    places = {
+        (0, 2): (3, 0),
+        (0, 0): (3, 3),
+        (0, 3): (5, 0),
+        (0, 1): (6, 0),
+        (1, 1): (6, 2),
+        (1, 2): (7, 0),
+        (1, 0): (7, 3),
+        (1, 3): (8, 0),
+    }
+    return band, {key: (row * band, col * band) for key, (row, col) in places.items()}
+
+
+MEAN_BANDS = (0, 1, 2, 4)
+READY = ((0,), (1,), (2, 3), (4, 5, 6, 7, 8))
+PACKED_BANDS = 9
+
+
+def add_band(part, tiles, index):
     order = part.shape[1]
     band, pieces = stat_pieces(order)
-    for kind, index, row, col in pieces:
-        width = (index + 1) * band
-        if kind == 0:
-            term = lax.dot_general(
-                tile[index * band : (index + 1) * band, :],
-                tile[0:width, :],
-                (((1,), (1,)), ((), ())),
+    rows = slice(index * band, (index + 1) * band)
+
+    def store(key, terms):
+        row, col = pieces[key]
+        total = sum(terms[1:], terms[0])
+        part[row : row + band, col : col + total.shape[1]] = total
+
+    mean = [tile[rows, :].astype(F32) for tile in tiles]
+    start = MEAN_BANDS[index] * band
+    part[start : start + band, :] = sum(mean[1:], mean[0])
+    width = (index + 1) * band
+    store(
+        (0, index),
+        [
+            lax.dot_general(
+                tile[rows, :], tile[0:width, :], (((1,), (1,)), ((), ())),
                 preferred_element_type=F32,
             )
-        else:
-            term = lax.dot_general(
-                tile[:, index * band : (index + 1) * band],
-                tile[:, 0:width],
-                (((0,), (0,)), ((), ())),
-                preferred_element_type=F32,
-            )
-        place = (slice(row, row + band), slice(col, col + width))
-        part[place] = term if first else part[place] + term
-    place = (slice(5 * band, 5 * band + order), slice(0, order))
-    term = tile[...].astype(F32)
-    part[place] = term if first else part[place] + term
+            for tile in tiles
+        ],
+    )
+    if index < BANDS - 1:
+        return
+    for other in range(BANDS):
+        width = (other + 1) * band
+        store(
+            (1, other),
+            [
+                lax.dot_general(
+                    tile[:, other * band : width], tile[:, 0:width], (((0,), (0,)), ((), ())),
+                    preferred_element_type=F32,
+                )
+                for tile in tiles
+            ],
+        )
 
 
 def sum_kernel(
@@ -67,9 +84,9 @@
     core = lax.rem(here_d, 2)
     chip = here_d // 2
     partner = here_d + 1 - 2 * core
-    rows = part.shape[0]
-    half = rows // 2
-    size = half // (2 * chunks)
+    last = chips - 1
+    band = part.shape[0] // chunks
+    size = band // 4
 
     barrier = pltpu.get_barrier_semaphore()
     for step in range(1, trials_n):
@@ -88,26 +105,24 @@
     neighbours = jnp.where(chip > 0, 1, 0) + jnp.where(chip < chips - 1, 1, 0)
     pl.semaphore_wait(barrier, trials_n + neighbours)
 
-    def grad_copy(step):
+    def grad_copy(step, index):
         peer = lax.rem(here_t + step, trials_n)
-        return pltpu.make_async_remote_copy(
-            src_ref=grads.at[peer],
-            dst_ref=mine.at[step - 1],
-            send_sem=grad_send.at[step - 1],
-            recv_sem=grad_recv.at[step - 1],
+        band_rows = pl.ds(index * band, band)
+        return pltpu.make_async_remote_copy(
+            src_ref=grads.at[peer, band_rows],
+            dst_ref=mine.at[step - 1, band_rows],
+            send_sem=grad_send.at[step - 1, index],
+            recv_sem=grad_recv.at[step - 1, index],
             device_id=(peer, here_d),
             device_id_type=MESH,
         )
 
-    for step in range(1, trials_n):
-        grad_copy(step).start()
-    add_tile(part, grads.at[here_t], True)
-    for step in range(1, trials_n):
-        grad_copy(step).wait_recv()
-        add_tile(part, mine.at[step - 1], False)
+    for index in range(BANDS):
+        for step in range(1, trials_n):
+            grad_copy(step, index).start()
 
     def chunk_at(owner, way, k):
-        return pl.ds(pl.multiple_of(owner * half + (way * chunks + k) * size, 8), size)
+        return pl.ds(pl.multiple_of(k * band + (owner * 2 + way) * size, 8), size)
 
     def swap_copy(way, k):
         return pltpu.make_async_remote_copy(
@@ -119,23 +134,37 @@
             device_id_type=MESH,
         )
 
+    owner = (chips // 2, chips // 2 - 1)
+    farthest = chips // 2
+
     def pass_copy(way, k):
+        side = jnp.where(chip < owner[way], 0, 1)
         return pltpu.make_async_remote_copy(
             src_ref=outgoing.at[way, k],
-            dst_ref=passed.at[way, k],
+            dst_ref=passed.at[way, side, k],
             send_sem=pass_send.at[way, k],
-            recv_sem=pass_recv.at[way, k],
-            device_id=(here_t, here_d + 2 - 4 * way),
-            device_id_type=MESH,
-        )
-
-    def back_copy(way, k):
+            recv_sem=pass_recv.at[way, side, k],
+            device_id=(here_t, here_d + 2 - 4 * side),
+            device_id_type=MESH,
+        )
+
+    def passed_from(way, side, k):
+        return pltpu.make_async_remote_copy(
+            src_ref=outgoing.at[way, k],
+            dst_ref=passed.at[way, side, k],
+            send_sem=pass_send.at[way, k],
+            recv_sem=pass_recv.at[way, side, k],
+            device_id=(here_t, here_d - 2 + 4 * side),
+            device_id_type=MESH,
+        )
+
+    def back_copy(way, side, k):
         return pltpu.make_async_remote_copy(
             src_ref=total.at[chunk_at(core, way, k)],
             dst_ref=total.at[chunk_at(core, way, k)],
-            send_sem=back_send.at[way, k],
+            send_sem=back_send.at[way, side, k],
             recv_sem=back_recv.at[way, k],
-            device_id=(here_t, here_d - 2 + 4 * way),
+            device_id=(here_t, here_d - 2 + 4 * side),
             device_id_type=MESH,
         )
 
@@ -159,75 +188,100 @@
             device_id_type=MESH,
         )
 
-    order = [(way, k) for k in range(chunks) for way in range(2)]
-    is_start = (chip == 0, chip == chips - 1)
-    is_end = (chip == chips - 1, chip == 0)
-
-    for way, k in order:
-        swap_copy(way, k).start()
-    last = chips - 1
-    distance = (chip, last - chip)
+    def sends_back(way):
+        return (
+            (chip <= owner[way]) & (chip > 0),
+            (chip >= owner[way]) & (chip < last),
+        )
+
+    def send_back(way, k):
+        for side in range(2):
+
+            @pl.when(sends_back(way)[side])
+            def _():
+                back_copy(way, side, k).start()
+
+        share_copy(way, k).start()
 
     def reduce_chunk(way, k):
         swap_copy(way, k).wait_recv()
         outgoing[way, k] = part[chunk_at(core, way, k), :] + swap[way, k]
-
-        @pl.when(jnp.logical_not(is_start[way]))
-        def _():
-            pass_copy(way, k).wait_recv()
-            outgoing[way, k] = outgoing[way, k] + passed[way, k]
-
-        @pl.when(jnp.logical_not(is_end[way]))
+        arrives = ((chip > 0) & (chip <= owner[way]), (chip < last) & (chip >= owner[way]))
+        for side in range(2):
+
+            @pl.when(arrives[side])
+            def _():
+                passed_from(way, side, k).wait_recv()
+                outgoing[way, k] = outgoing[way, k] + passed[way, side, k]
+
+        @pl.when(chip != owner[way])
         def _():
             pass_copy(way, k).start()
 
-        @pl.when(is_end[way])
+        @pl.when(chip == owner[way])
         def _():
             total[chunk_at(core, way, k), :] = outgoing[way, k]
-            back_copy(way, k).start()
-            share_copy(way, k).start()
+            send_back(way, k)
 
     def return_chunk(way, k):
-        back_copy(way, k).wait_recv()
-
-        @pl.when(jnp.logical_not(is_start[way]))
-        def _():
-            back_copy(way, k).start()
-
-        share_copy(way, k).start()
-
-    @pl.loop(0, chunks + 2 * last)
-    def _(step):
+        back_copy(way, 0, k).wait_recv()
+        send_back(way, k)
+
+    def chain_step(step):
         for way in range(2):
-            k = step - distance[way]
+            hops = jnp.where(
+                chip < owner[way], chip, jnp.where(chip > owner[way], last - chip, farthest)
+            )
+            k = step - hops
 
             @pl.when((k >= 0) & (k < chunks))
             def _():
                 reduce_chunk(way, k)
 
         for way in range(2):
-            k = step - last - distance[1 - way]
-
-            @pl.when((k >= 0) & (k < chunks) & jnp.logical_not(is_end[way]))
+            away = jnp.where(chip < owner[way], owner[way] - chip, chip - owner[way])
+            k = step - farthest - away
+
+            @pl.when((k >= 0) & (k < chunks) & (away > 0))
             def _():
                 return_chunk(way, k)
 
+    tiles = [grads.at[here_t]] + [mine.at[step] for step in range(trials_n - 1)]
+    for index in range(BANDS):
+        for step in range(1, trials_n):
+            grad_copy(step, index).wait_recv()
+        add_band(part, tiles, index)
+        for k in READY[index]:
+            for way in range(2):
+                swap_copy(way, k).start()
+        if index < BANDS - 1:
+            for k in READY[index]:
+                chain_step(k)
+
+    @pl.loop(READY[-1][0], chunks + 2 * farthest)
+    def _(step):
+        chain_step(step)
+
+    order = [(way, k) for k in range(chunks) for way in range(2)]
     for way, k in order:
         shared_by_partner(way, k).wait_recv()
     for way, k in order:
         swap_copy(way, k).wait_send()
         share_copy(way, k).wait_send()
 
-        @pl.when(jnp.logical_not(is_end[way]))
+        @pl.when(chip != owner[way])
         def _():
             pass_copy(way, k).wait_send()
 
-        @pl.when(jnp.logical_not(is_start[way]))
-        def _():
-            back_copy(way, k).wait_send()
-
-    for step in range(1, trials_n):
-        grad_copy(step).wait_send()
+        for side in range(2):
+
+            @pl.when(sends_back(way)[side])
+            def _():
+                back_copy(way, side, k).wait_send()
+
+    for index in range(BANDS):
+        for step in range(1, trials_n):
+            grad_copy(step, index).wait_send()
 
 
 def split(value):
@@ -273,9 +327,8 @@
     weight = 1.0 / (devices * order)
 
     for kind in range(2):
-        for piece_kind, index, row, col in pieces:
-            if piece_kind != kind:
-                continue
+        for index in range(BANDS):
+            row, col = pieces[kind, index]
             for other in range(index + 1):
                 block = packed[row : row + band, col + other * band : col + (other + 1) * band]
                 block = block * weight
@@ -301,7 +354,9 @@
         )
         root_high[kind], root_low[kind] = split(root)
 
-    average = packed[5 * band : 5 * band + order, :] * (1.0 / devices)
+    average = jnp.concatenate(
+        [packed[row * band : (row + 1) * band, :] for row in MEAN_BANDS], axis=0
+    ) * (1.0 / devices)
     middle = product((root_high[0], root_low[0]), split(average))
     raw = product(split(middle), (root_high[1], root_low[1]))
     count = order * order
@@ -369,28 +424,36 @@
     settings = exponents.shape[0]
     tiles, order = grads.shape[1], grads.shape[-1]
     assert tiles == trials_n and data_n >= settings and data_n % 2 == 0
-    rows = packed_rows(order)
-    size = rows // (4 * CHUNKS)
+    rows = PACKED_BANDS * (order // BANDS)
+    size = order // BANDS // 4
     in_vmem = pl.BlockSpec(memory_space=pltpu.VMEM)
     in_smem = pl.BlockSpec(memory_space=pltpu.SMEM)
     dma = pltpu.SemaphoreType.DMA
-    pairs = dma((2, CHUNKS))
+    pairs = dma((2, PACKED_BANDS))
+    sides = dma((2, 2, PACKED_BANDS))
 
     packed = pl.pallas_call(
-        functools.partial(sum_kernel, trials_n, data_n, CHUNKS),
+        functools.partial(sum_kernel, trials_n, data_n, PACKED_BANDS),
         out_shape=jax.ShapeDtypeStruct((rows, order), F32),
         in_specs=[in_vmem],
         out_specs=in_vmem,
         scratch_shapes=[
             pltpu.VMEM((trials_n - 1, order, order), BF16),
             pltpu.VMEM((rows, order), F32),
-            pltpu.VMEM((2, CHUNKS, size, order), F32),
-            pltpu.VMEM((2, CHUNKS, size, order), F32),
-            pltpu.VMEM((2, CHUNKS, size, order), F32),
-            dma((trials_n - 1,)),
-            dma((trials_n - 1,)),
-        ]
-        + [pairs] * 8,
+            pltpu.VMEM((2, PACKED_BANDS, size, order), F32),
+            pltpu.VMEM((2, 2, PACKED_BANDS, size, order), F32),
+            pltpu.VMEM((2, PACKED_BANDS, size, order), F32),
+            dma((trials_n - 1, BANDS)),
+            dma((trials_n - 1, BANDS)),
+            pairs,
+            pairs,
+            pairs,
+            sides,
+            sides,
+            pairs,
+            pairs,
+            pairs,
+        ],
         compiler_params=pltpu.CompilerParams(
             collective_id=0, has_side_effects=True, vmem_limit_bytes=40 * 1024 * 1024
         ),

time: 99.6 us -> 87.7 us (0.88)
  Pallas kernels: 97 us -> 85.1 us
    pallas_call x1, Pallas kernels: 75 us -> 62.2 us  [per_device(): pl.pallas_call(functools.partial(sum_kernel, trials_n, data_n, PACKED_BAN...]
where the time goes in v4:
time: 87.7 us; the launch traced here: 87.5 us
  Pallas kernels  85.1 us (97%)
  local copies, waits for them, and re-layouts  2.42 us (3%)
    pallas_call x1, Pallas kernels, per_device(): pl.pallas_call(functools.partial(sum_kernel, trials_n, data_n, PACKED_BAN...  62.2 us
    pallas_call x1, Pallas kernels, per_device(): pl.pallas_call(functools.partial(update_kernel, trials_n, data_n, setting...  22.9 us
    unnamed x7, local copies, waits for them, and re-layouts  2.42 us

profile of v4, /device:TPU:0, one launch (start us, length us, event | category | flops | bytes accessed | tf_op | source)
XLA Modules:
  0.0 87.5 jit_solution(10090304168041016359)
XLA Ops:
  0.0 0.0 copy-start.2
  0.0 0.0 copy-start.1
  0.0 0.0 copy-start
  0.0 1.6 %copy-done = bf16[1,4,512,512]{3,2,1,0:T(8,128)(2,1)S(1)} copy-done((bf16[1,4,512,512]{3,2,1,0:T(8,128)(2,1)S(1)}, bf16[1,4,512,512]{3,2,1,0:T(8,128)(2,1)}, u32[]{:S(2)}) %copy-start) | copy-done | bytes 2097176
  1.6 62.2 %shard_map.37.packed = f32[1152,512]{1,0:T(8,128)S(1)} custom-call(bf16[4,512,512]{2,1,0:T(8,128)(2,1)S(1)} %bitcast.1), custom_call_target="tpu_custom_call" | custom-call | tf_op jit(solution)/shard_map/pallas_call | solution.py:435
  63.8 0.0 copy-done.2
  63.8 0.0 copy-done.1
  63.8 22.9 %shard_map.38 = bf16[8,4,64,128]{3,2,1,0:T(8,128)(2,1)S(1)} custom-call(f32[1152,512]{1,0:T(8,128)S(1)} %shard_map.37.packed, s32[8]{0:T(128)S(1)} %copy-done.1, f32[8]{0:T(128)S(1)} %copy-done.2), custom_call_target="tpu_custom_call" | custom-call | tf_op jit(solution)/shard_map/pallas_call | solution.py:462
  86.7 0.8 copy.5
Async XLA Ops:
  0.0 63.8 %copy-start.2 = (f32[8]{0:T(128)S(1)}, f32[8]{0:T(128)}, u32[]{:S(2)}) copy-start(f32[8]{0:T(128)} %dampings.1) | copy-start | bytes 100
  0.0 63.8 %copy-start.1 = (s32[8]{0:T(128)S(1)}, s32[8]{0:T(128)}, u32[]{:S(2)}) copy-start(s32[8]{0:T(128)} %exponents.1) | copy-start | bytes 100
  0.0 1.6 %copy-start = (bf16[1,4,512,512]{3,2,1,0:T(8,128)(2,1)S(1)}, bf16[1,4,512,512]{3,2,1,0:T(8,128)(2,1)}, u32[]{:S(2)}) copy-start(bf16[1,4,512,512]{3,2,1,0:T(8,128)(2,1)} %param.3) | copy-start | bytes 6291460

commit v5 on v4

--- a/solution.py
+++ b/solution.py
@@ -18,17 +18,18 @@
     places = {
         (0, 2): (3, 0),
         (0, 0): (3, 3),
-        (0, 3): (5, 0),
-        (0, 1): (6, 0),
-        (1, 1): (6, 2),
-        (1, 2): (7, 0),
-        (1, 0): (7, 3),
-        (1, 3): (8, 0),
+        (0, 3): (4, 0),
+        (0, 1): (5, 0),
+        (1, 1): (5, 2),
+        (1, 2): (6, 0),
+        (1, 0): (6, 3),
+        (1, 3): (7, 0),
     }
     return band, {key: (row * band, col * band) for key, (row, col) in places.items()}
 
 
-MEAN_BANDS = (0, 1, 2, 4)
+MEAN_BANDS = (0, 1, 2, 8)
+STAT_ENDS = (5, 7)
 READY = ((0,), (1,), (2, 3), (4, 5, 6, 7, 8))
 PACKED_BANDS = 9
 
@@ -73,13 +74,29 @@
         )
 
 
-def sum_kernel(
-    trials_n, data_n, chunks, grads, total, mine, part, swap, passed, outgoing,
-    grad_send, grad_recv, swap_send, swap_recv, pass_send, pass_recv,
-    back_send, back_recv, share_send, share_recv,
+def split(value):
+    high = value.astype(BF16)
+    return high, (value - high.astype(F32)).astype(BF16)
+
+
+def product(first, second):
+    def dot(a, b):
+        return jnp.dot(a, b, preferred_element_type=F32)
+
+    return dot(first[0], second[0]) + (dot(first[0], second[1]) + dot(first[1], second[0]))
+
+
+def update_kernel(
+    trials_n, data_n, settings, chunks, grads, exponents, dampings, out,
+    tile, mine, part, swap, passed, outgoing, total, stat, square, turned, root, finished,
+    tile_sem, grad_send, grad_recv, swap_send, swap_recv, pass_send, pass_recv,
+    back_send, back_recv, share_send, share_recv, own_sem, send_sem, recv_sem,
 ):
     here_t = lax.axis_index("trial")
     here_d = lax.axis_index("dp")
+    devices = trials_n * data_n
+    here = here_t * data_n + here_d
+    setting = lax.rem(here_d, settings)
     chips = data_n // 2
     core = lax.rem(here_d, 2)
     chip = here_d // 2
@@ -88,22 +105,18 @@
     band = part.shape[0] // chunks
     size = band // 4
 
+    own_tile = pltpu.make_async_copy(grads.at[here_t], tile, tile_sem)
+    own_tile.start()
     barrier = pltpu.get_barrier_semaphore()
-    for step in range(1, trials_n):
-        peer = lax.rem(here_t + step, trials_n)
-        pl.semaphore_signal(barrier, inc=1, device_id=(peer, here_d), device_id_type=MESH)
-    pl.semaphore_signal(barrier, inc=1, device_id=(here_t, partner), device_id_type=MESH)
-
-    @pl.when(chip > 0)
-    def _():
-        pl.semaphore_signal(barrier, inc=1, device_id=(here_t, here_d - 2), device_id_type=MESH)
-
-    @pl.when(chip < chips - 1)
-    def _():
-        pl.semaphore_signal(barrier, inc=1, device_id=(here_t, here_d + 2), device_id_type=MESH)
-
-    neighbours = jnp.where(chip > 0, 1, 0) + jnp.where(chip < chips - 1, 1, 0)
-    pl.semaphore_wait(barrier, trials_n + neighbours)
+
+    @pl.loop(1, devices)
+    def _(step):
+        peer = lax.rem(here + step, devices)
+        pl.semaphore_signal(
+            barrier, inc=1, device_id=(peer // data_n, lax.rem(peer, data_n)), device_id_type=MESH
+        )
+
+    pl.semaphore_wait(barrier, devices - 1)
 
     def grad_copy(step, index):
         peer = lax.rem(here_t + step, trials_n)
@@ -246,7 +259,8 @@
             def _():
                 return_chunk(way, k)
 
-    tiles = [grads.at[here_t]] + [mine.at[step] for step in range(trials_n - 1)]
+    own_tile.wait()
+    tiles = [tile] + [mine.at[step] for step in range(trials_n - 1)]
     for index in range(BANDS):
         for step in range(1, trials_n):
             grad_copy(step, index).wait_recv()
@@ -258,107 +272,84 @@
             for k in READY[index]:
                 chain_step(k)
 
-    @pl.loop(READY[-1][0], chunks + 2 * farthest)
-    def _(step):
-        chain_step(step)
-
-    order = [(way, k) for k in range(chunks) for way in range(2)]
-    for way, k in order:
-        shared_by_partner(way, k).wait_recv()
-    for way, k in order:
-        swap_copy(way, k).wait_send()
-        share_copy(way, k).wait_send()
-
-        @pl.when(chip != owner[way])
-        def _():
-            pass_copy(way, k).wait_send()
-
-        for side in range(2):
-
-            @pl.when(sends_back(way)[side])
-            def _():
-                back_copy(way, side, k).wait_send()
-
-    for index in range(BANDS):
-        for step in range(1, trials_n):
-            grad_copy(step, index).wait_send()
-
-
-def split(value):
-    high = value.astype(BF16)
-    return high, (value - high.astype(F32)).astype(BF16)
-
-
-def product(first, second):
-    def dot(a, b):
-        return jnp.dot(a, b, preferred_element_type=F32)
-
-    return dot(first[0], second[0]) + (dot(first[0], second[1]) + dot(first[1], second[0]))
-
-
-def update_kernel(
-    trials_n, data_n, settings, packed, exponents, dampings, out,
-    stat, factor, square, cube, root_high, root_low, finished, own_sem, send_sem, recv_sem,
-):
-    here_t = lax.axis_index("trial")
-    here_d = lax.axis_index("dp")
-    devices = trials_n * data_n
-    here = here_t * data_n + here_d
-    order = packed.shape[1]
-    setting = lax.rem(here_d, settings)
-
-    barrier = pltpu.get_barrier_semaphore()
-
-    @pl.loop(1, devices)
-    def _(step):
-        peer = lax.rem(here + step, devices)
-        pl.semaphore_signal(
-            barrier, inc=1, device_id=(peer // data_n, lax.rem(peer, data_n)), device_id_type=MESH
-        )
-
-    band, pieces = stat_pieces(order)
     exponent = jnp.full((1, 1), exponents[setting], jnp.int32)
     damping = jnp.full((1, 1), dampings[setting], F32)
     order_f = exponent.astype(F32)
-    eye = (
-        lax.broadcasted_iota(jnp.int32, (order, order), 0)
-        == lax.broadcasted_iota(jnp.int32, (order, order), 1)
-    )
+    ratio = (order_f + 1.0) / order_f
+    order = total.shape[1]
+    _, pieces = stat_pieces(order)
     weight = 1.0 / (devices * order)
 
-    for kind in range(2):
+    def begin_root(kind):
         for index in range(BANDS):
             row, col = pieces[kind, index]
             for other in range(index + 1):
-                block = packed[row : row + band, col + other * band : col + (other + 1) * band]
+                block = total[row : row + band, col + other * band : col + (other + 1) * band]
                 block = block * weight
+                if other == index:
+                    eye = lax.broadcasted_iota(jnp.int32, (band, band), 0) == (
+                        lax.broadcasted_iota(jnp.int32, (band, band), 1)
+                    )
+                    block = block + jnp.where(eye, damping, 0.0)
                 stat[index * band : (index + 1) * band, other * band : (other + 1) * band] = block
                 if other < index:
                     stat[other * band : (other + 1) * band, index * band : (index + 1) * band] = (
                         block.T
                     )
-        shifted = stat[...] + jnp.where(eye, damping, 0.0)
-        norm = jnp.sqrt(jnp.sum(shifted * shifted, keepdims=True) + 1e-06)
+        norm = jnp.sqrt(jnp.sum(stat[...] * stat[...], keepdims=True) + 1e-06)
         scaling = (1.0 + order_f) / (2.0 * norm)
-        factor[...] = (jnp.where(eye, order_f + 1.0, 0.0) - scaling * shifted) / order_f
-        factor_parts = split(factor[...])
-        square[...] = product(factor_parts, factor_parts)
-        square_parts = split(square[...])
-        cube[...] = product(square_parts, factor_parts)
-        low = jnp.where(exponent == 2, factor[...], square[...])
-        high = jnp.where(exponent == 2, square[...], cube[...])
-        outer = jnp.where(exponent == 4, cube[...], square[...])
-        tail = product(split(outer), split(order_f * high - (order_f + 1.0) * low))
-        root = (jnp.exp(jnp.log(scaling) / order_f) / order_f) * (
-            (order_f + 1.0) * factor[...] + tail
-        )
-        root_high[kind], root_low[kind] = split(root)
+        stat[...] = stat[...] * (scaling / order_f)
+        parts = split(stat[...])
+        square[...] = product(parts, parts)
+        return jnp.exp(jnp.log(scaling) / order_f)
+
+    def turn_root():
+        once = ratio * stat[...] - square[...]
+        twice = ratio * once - product(split(stat[...]), split(once))
+        turned[...] = jnp.where(exponent == 2, once, twice)
+
+    def end_root(kind):
+        short = (2.0 * ratio) * stat[...] - square[...]
+        taken = jnp.where(exponent == 4, ratio * short + turned[...], short)
+        power = jnp.where(exponent == 4, ratio * ratio * ratio, ratio * ratio)
+        rest = product(split(taken), split(turned[...])) - power * turned[...]
+        root[kind] = rest - ratio * stat[...]
+
+    sent = [(way, k) for k in range(chunks) for way in range(2)]
+
+    def wait_shared(first, stop):
+        for k in range(first, stop):
+            for way in range(2):
+                shared_by_partner(way, k).wait_recv()
+
+    left_stop = STAT_ENDS[0] + 1
+    right_stop = STAT_ENDS[1] + 1
+    steps = chunks + 2 * farthest
+
+    @pl.loop(READY[-1][0], left_stop + 2 * farthest)
+    def _(step):
+        chain_step(step)
+
+    wait_shared(0, left_stop)
+    left_scale = begin_root(0)
+    chain_step(left_stop + 2 * farthest)
+    turn_root()
+    chain_step(left_stop + 2 * farthest + 1)
+    end_root(0)
+    chain_step(steps - 1)
+    wait_shared(left_stop, right_stop)
+    right_scale = begin_root(1)
+    turn_root()
+    end_root(1)
+    wait_shared(right_stop, chunks)
 
     average = jnp.concatenate(
-        [packed[row * band : (row + 1) * band, :] for row in MEAN_BANDS], axis=0
+        [total[row * band : (row + 1) * band, :] for row in MEAN_BANDS], axis=0
     ) * (1.0 / devices)
-    middle = product((root_high[0], root_low[0]), split(average))
-    raw = product(split(middle), (root_high[1], root_low[1]))
+    middle = left_scale * (
+        ratio * ratio * average + product(split(root[0]), split(average))
+    )
+    raw = right_scale * (ratio * ratio * middle + product(split(middle), split(root[1])))
     count = order * order
     target = jnp.sqrt(jnp.sum(average * average, keepdims=True) / count)
     spread = jnp.sqrt(jnp.sum(raw * raw, keepdims=True) / count + 1e-06)
@@ -370,8 +361,6 @@
                 d * row_share : (d + 1) * row_share, t * col_share : (t + 1) * col_share
             ].astype(BF16)
 
-    pl.semaphore_wait(barrier, devices - 1)
-
     def block_copy(peer):
         peer_t, peer_d = peer // data_n, lax.rem(peer, data_n)
         return pltpu.make_async_remote_copy(
@@ -415,6 +404,24 @@
         @pl.loop(1, devices)
         def _(step):
             block_copy(lax.rem(here + step, devices)).wait_send()
+
+    for way, k in sent:
+        swap_copy(way, k).wait_send()
+        share_copy(way, k).wait_send()
+
+        @pl.when(chip != owner[way])
+        def _():
+            pass_copy(way, k).wait_send()
+
+        for side in range(2):
+
+            @pl.when(sends_back(way)[side])
+            def _():
+                back_copy(way, side, k).wait_send()
+
+    for index in range(BANDS):
+        for step in range(1, trials_n):
+            grad_copy(step, index).wait_send()
 
 
 def per_device(grads, exponents, dampings):
@@ -428,21 +435,32 @@
     size = order // BANDS // 4
     in_vmem = pl.BlockSpec(memory_space=pltpu.VMEM)
     in_smem = pl.BlockSpec(memory_space=pltpu.SMEM)
+    in_place = pl.BlockSpec(memory_space=pl.ANY)
     dma = pltpu.SemaphoreType.DMA
     pairs = dma((2, PACKED_BANDS))
     sides = dma((2, 2, PACKED_BANDS))
-
-    packed = pl.pallas_call(
-        functools.partial(sum_kernel, trials_n, data_n, PACKED_BANDS),
-        out_shape=jax.ShapeDtypeStruct((rows, order), F32),
-        in_specs=[in_vmem],
+    whole = pltpu.VMEM((order, order), F32)
+    row_share, col_share = order // data_n, order // trials_n
+
+    return pl.pallas_call(
+        functools.partial(update_kernel, trials_n, data_n, settings, PACKED_BANDS),
+        out_shape=jax.ShapeDtypeStruct((settings, tiles, row_share, col_share), BF16),
+        in_specs=[in_place, in_smem, in_smem],
         out_specs=in_vmem,
         scratch_shapes=[
+            pltpu.VMEM((order, order), BF16),
             pltpu.VMEM((trials_n - 1, order, order), BF16),
             pltpu.VMEM((rows, order), F32),
             pltpu.VMEM((2, PACKED_BANDS, size, order), F32),
             pltpu.VMEM((2, 2, PACKED_BANDS, size, order), F32),
             pltpu.VMEM((2, PACKED_BANDS, size, order), F32),
+            pltpu.VMEM((rows, order), F32),
+            whole,
+            whole,
+            whole,
+            pltpu.VMEM((2, order, order), F32),
+            pltpu.VMEM((trials_n, data_n, row_share, col_share), BF16),
+            dma,
             dma((trials_n - 1, BANDS)),
             dma((trials_n - 1, BANDS)),
             pairs,
@@ -453,36 +471,14 @@
             pairs,
             pairs,
             pairs,
-        ],
-        compiler_params=pltpu.CompilerParams(
-            collective_id=0, has_side_effects=True, vmem_limit_bytes=40 * 1024 * 1024
-        ),
-    )(grads[0])
-
-    out = pl.pallas_call(
-        functools.partial(update_kernel, trials_n, data_n, settings),
-        out_shape=jax.ShapeDtypeStruct(
-            (settings, tiles, order // data_n, order // trials_n), BF16
-        ),
-        in_specs=[in_vmem, in_smem, in_smem],
-        out_specs=in_vmem,
-        scratch_shapes=[
-            pltpu.VMEM((order, order), F32),
-            pltpu.VMEM((order, order), F32),
-            pltpu.VMEM((order, order), F32),
-            pltpu.VMEM((order, order), F32),
-            pltpu.VMEM((2, order, order), BF16),
-            pltpu.VMEM((2, order, order), BF16),
-            pltpu.VMEM((trials_n, data_n, order // data_n, order // trials_n), BF16),
             dma,
             dma((devices,)),
             dma((settings, trials_n)),
         ],
         compiler_params=pltpu.CompilerParams(
-            collective_id=1, has_side_effects=True, vmem_limit_bytes=40 * 1024 * 1024
+            collective_id=0, has_side_effects=True, vmem_limit_bytes=48 * 1024 * 1024
         ),
-    )(packed, exponents, dampings)
-    return out
+    )(grads[0], exponents, dampings)
 
 
 def solution(mesh):

time: 87.7 us -> 85.1 us (0.970)
  Pallas kernels: 85.1 us -> 81.2 us
  local copies, waits for them, and re-layouts: 2.42 us -> 3.7 us
    pallas_call x1 -> x0, Pallas kernels: 62.2 us -> none  [per_device(): pl.pallas_call(functools.partial(sum_kernel, trials_n, data_n, PACKED_BAN...]
    pallas_call x1, Pallas kernels: 22.9 us -> 81.2 us  [per_device(): pl.pallas_call(functools.partial(update_kernel, trials_n, data_n, setting...]
    unnamed x7, local copies, waits for them, and re-layouts: 2.42 us -> 3.7 us
where the time goes in v5:
time: 85.1 us; the launch traced here: 84.9 us
  Pallas kernels  81.2 us (95%)
  local copies, waits for them, and re-layouts  3.7 us (4%)
    pallas_call x1, Pallas kernels, per_device(): pl.pallas_call(functools.partial(update_kernel, trials_n, data_n, setting...  81.2 us
    unnamed x7, local copies, waits for them, and re-layouts  3.7 us

profile of v5, /device:TPU:0, one launch (start us, length us, event | category | flops | bytes accessed | tf_op | source)
XLA Modules:
  0.0 84.9 jit_solution(5052010663817512402)
XLA Ops:
  0.0 0.0 copy-start
  0.0 1.6 %copy-done = bf16[1,4,512,512]{3,2,1,0:T(8,128)(2,1)S(1)} copy-done((bf16[1,4,512,512]{3,2,1,0:T(8,128)(2,1)S(1)}, bf16[1,4,512,512]{3,2,1,0:T(8,128)(2,1)}, u32[]{:S(2)}) %copy-start) | copy-done | bytes 2097176
  1.6 0.0 copy-start.1
  1.6 0.7 copy-done.1
  2.2 0.0 copy-start.2
  2.2 0.7 copy-done.2
  2.9 81.2 %shard_map.37 = bf16[8,4,64,128]{3,2,1,0:T(8,128)(2,1)S(1)} custom-call(bf16[4,512,512]{2,1,0:T(8,128)(2,1)S(1)} %bitcast.1, s32[8]{0:T(128)S(1)} %copy-done.1, f32[8]{0:T(128)S(1)} %copy-done.2), custom_call_target="tpu_custom_call" | custom-call | tf_op jit(solution)/shard_map/pallas_call | solution.py:445
  84.1 0.8 copy.5
Async XLA Ops:
  0.0 1.6 %copy-start = (bf16[1,4,512,512]{3,2,1,0:T(8,128)(2,1)S(1)}, bf16[1,4,512,512]{3,2,1,0:T(8,128)(2,1)}, u32[]{:S(2)}) copy-start(bf16[1,4,512,512]{3,2,1,0:T(8,128)(2,1)} %param.3) | copy-start | bytes 6291460
  1.6 0.7 copy-start.1
  2.2 0.7 copy-start.2
